TPU v7x, 32 devices: a whole 2x2x4 slice. The times are simulated.
32 devices in a mesh: wa: 8 (over z, x), af: 4 (over y, core).
Axes of the slice: x: 2, y: 2, z: 4, core: 2. Of those that a mesh axis runs over, the one named last changes fastest.
Arguments:
- spectra: bfloat16 [80, 80, 128], P('wa', None, 'af'), may hold values from -6 to 6
- legendre: bfloat16 [80, 80, 8], P('wa', 'af'), may hold values from -0.625 to 0.625
- wave_of_slot: int32 [80], replicated, may hold values from 0 to 79, each once
- row_points: int32 [8], P('wa'), may hold values from 2560 to 5120, as said below
- row_weight: float32 [8], P('wa'), may hold values from 0.1 to 1.5, as said below
- soil_water: float32 [8, 4, 5120], P('wa', None, 'af'), may hold values from 0.02 to 0.48
- land_mask: int32 [8, 5120], P('wa', 'af'), may hold values 0 or 1
- soil_type: int32 [8, 5120], P('wa', 'af'), may hold values from 0 to 6
- plant_type: int32 [8, 5120], P('wa', 'af'), may hold values from 0 to 19
- soil_params: float32 [2, 7], replicated, may hold values from 0 to 1
- root_profile: float32 [20, 4], replicated, may hold values from 0.1 to 10
Outputs:
- grid_fields: bfloat16 [8, 64, 5120], P('wa', None, 'af')
- uptake: float32 [8, 4, 5120], P('wa', None, 'af')
- spectral_fluxes: float32 [80, 8, 80], P('wa', None, 'af')
Inputs may be any that keep to these rules, and one draw needn't show every extreme that they name: `wave_of_slot`: each slot number from 0 to 79 is named once. `row_points`: every count is a multiple of 4; some row has exactly 5120 points and some row exactly 2560. `row_weight`: positive weights.
All inputs are finite; a program needn't handle non-finite values. No bound on the sum of `land_mask` on one device may be relied on, other than what follows from the above.
Results may differ from a plain program's by a relative error of at most 0.009.
Values may be sent and summed in bfloat16 or wider, within the bound.
A program may use at most 64 MiB of HBM per device.

v0:
```python
import math

import jax
import jax.numpy as jnp
from jax import lax
from jax.sharding import PartitionSpec as P

LEVELS = 8
FLUXES = 4
SOIL_LAYERS = 4
SOIL_TYPES = 7
PLANT_TYPES = 20


TWO_PI = 2.0 * math.pi
DEPTHS = (0.07, 0.21, 0.72, 1.89)
UPTAKE_SHARE = 4.0


def wave_tables(wavenumbers, points, longitudes):
    phases = wavenumbers[None, :, None] * longitudes[None, None, :] % points[:, None, None]
    angles = phases.astype(jnp.float32) * TWO_PI / points.astype(jnp.float32)[:, None, None]
    inside = longitudes[None, None, :] < points[:, None, None]
    cosine_table = jnp.where(inside, jnp.cos(angles), 0.0)
    sine_table = jnp.where(inside, jnp.sin(angles), 0.0)
    return (cosine_table, sine_table)


def block_width():
    return 256


def synth_block(real_part, imag_part, cosine_table, sine_table, synth_scale):
    summed = jnp.einsum(
        "frm,rml->rfl", real_part, cosine_table, preferred_element_type=jnp.float32
    ) - jnp.einsum("frm,rml->rfl", imag_part, sine_table, preferred_element_type=jnp.float32)
    return (summed * synth_scale).astype(jnp.bfloat16)


def physics(
    grid_fields,
    longitudes,
    row_points,
    soil_water,
    land_mask,
    soil_type,
    plant_type,
    soil_params,
    root_profile,
):
    values = grid_fields.astype(jnp.float32)
    wind_u = values[:, LEVELS - 1, :]
    wind_v = values[:, 2 * LEVELS - 1, :]
    air_temp = values[:, 3 * LEVELS - 1, :]
    humidity = values[:, 4 * LEVELS - 1, :]
    skin_temp = values[:, 5 * LEVELS - 1, :]
    wind_speed = jnp.sqrt(1.0 + wind_u * wind_u + wind_v * wind_v)
    demand = 0.5 * wind_speed * jax.nn.softplus(air_temp - humidity)
    in_row = (longitudes[None, :] < row_points[:, None]).astype(jnp.float32)
    usable = in_row * land_mask.astype(jnp.float32)
    soil_onehot = (soil_type[:, :, None] == jnp.arange(SOIL_TYPES, dtype=jnp.int32)).astype(
        jnp.float32
    )
    wilting = 0.04 + 0.1 * jnp.sum(soil_onehot * soil_params[0], axis=-1)
    capacity = 0.3 + 0.15 * jnp.sum(soil_onehot * soil_params[1], axis=-1)
    fractions = root_profile / jnp.sum(root_profile, axis=1, keepdims=True)
    plant_onehot = (plant_type[:, :, None] == jnp.arange(PLANT_TYPES, dtype=jnp.int32)).astype(
        jnp.float32
    )
    stress = jnp.zeros_like(demand)
    reserve = jnp.zeros_like(demand)
    layer_terms = []
    for layer_num in range(SOIL_LAYERS):
        root_share = jnp.sum(plant_onehot * fractions[:, layer_num], axis=-1)
        moisture = soil_water[:, layer_num, :]
        factor = jnp.clip((moisture - wilting) / (capacity - wilting), 0.0, 1.0)
        layer_terms.append(usable * demand * root_share * factor)
        stress = stress + root_share * factor
        reserve = reserve + root_share * DEPTHS[layer_num] * jnp.maximum(moisture - wilting, 0.0)
    transpiration = usable * demand * stress
    available = usable * reserve
    other_fluxes = (
        in_row * wind_speed * (skin_temp - air_temp),
        in_row * wind_speed * wind_u,
        in_row * wind_speed * wind_v,
    )
    return (layer_terms, transpiration, available, other_fluxes)


def column_pass(
    real_part,
    imag_part,
    row_points,
    row_weight,
    wavenumbers,
    first_lon,
    soil_water,
    land_mask,
    soil_type,
    plant_type,
    soil_params,
    root_profile,
):
    lat_rows = row_points.shape[0]
    lon_count = soil_water.shape[2]
    total_waves = wavenumbers.shape[0]
    lon_block = block_width()
    synth_scale = 1.0 / math.sqrt(total_waves)
    cell_area = (row_weight / row_points.astype(jnp.float32))[:, None]
    field_count = real_part.shape[0]
    start = (
        jnp.zeros((lat_rows, field_count, lon_count), jnp.bfloat16),
        jnp.zeros((lat_rows, SOIL_LAYERS, lon_count), jnp.float32),
        jnp.zeros((), jnp.float32),
        jnp.zeros((), jnp.float32),
        jnp.zeros((lat_rows, FLUXES, 2, total_waves), jnp.float32),
    )

    def one_block(block_num, carry):
        grid_out, layer_out, demand_part, avail_part, running = carry
        offset = block_num * lon_block
        longitudes = first_lon + offset + jnp.arange(lon_block, dtype=jnp.int32)
        cosine_table, sine_table = wave_tables(wavenumbers, row_points, longitudes)
        block_grid = synth_block(
            real_part,
            imag_part,
            cosine_table.astype(jnp.bfloat16),
            sine_table.astype(jnp.bfloat16),
            synth_scale,
        )
        layer_terms, transpiration, available, other_fluxes = physics(
            block_grid,
            longitudes,
            row_points,
            lax.dynamic_slice_in_dim(soil_water, offset, lon_block, 2),
            lax.dynamic_slice_in_dim(land_mask, offset, lon_block, 1),
            lax.dynamic_slice_in_dim(soil_type, offset, lon_block, 1),
            lax.dynamic_slice_in_dim(plant_type, offset, lon_block, 1),
            soil_params,
            root_profile,
        )
        demand_part = demand_part + jnp.sum(cell_area * transpiration)
        avail_part = avail_part + jnp.sum(cell_area * available)
        values = jnp.stack(
            [transpiration, other_fluxes[0], other_fluxes[1], other_fluxes[2]], axis=1
        )
        real_coef = jnp.einsum(
            "rql,rml->rqm",
            values,
            cosine_table,
            precision=lax.Precision.HIGHEST,
            preferred_element_type=jnp.float32,
        )
        imag_coef = -jnp.einsum(
            "rql,rml->rqm",
            values,
            sine_table,
            precision=lax.Precision.HIGHEST,
            preferred_element_type=jnp.float32,
        )
        running = running + jnp.stack([real_coef, imag_coef], axis=2)
        grid_out = lax.dynamic_update_slice_in_dim(grid_out, block_grid, offset, 2)
        layer_out = lax.dynamic_update_slice_in_dim(
            layer_out, jnp.stack(layer_terms, axis=1), offset, 2
        )
        return (grid_out, layer_out, demand_part, avail_part, running)

    return lax.fori_loop(0, lon_count // lon_block, one_block, start)


def sum_rows(values):
    return lax.psum(values, "af")


def per_device(
    spectra,
    legendre,
    wave_of_slot,
    row_points,
    row_weight,
    soil_water,
    land_mask,
    soil_type,
    plant_type,
    soil_params,
    root_profile,
):
    slot_count = spectra.shape[0]
    total_waves = wave_of_slot.shape[0]
    group_cols = spectra.shape[2]
    group_fields = group_cols // 2
    lat_count = legendre.shape[2]
    lat_rows = row_points.shape[0]
    lon_count = soil_water.shape[2]
    wa_count = lax.axis_size("wa")
    af_count = lax.axis_size("af")
    my_waves = lax.dynamic_slice_in_dim(wave_of_slot, lax.axis_index("wa") * slot_count, slot_count)
    offsets = jnp.arange(spectra.shape[1], dtype=jnp.int32)
    kept_rows = offsets[None, :] < (total_waves - my_waves)[:, None]
    masked = jnp.where(kept_rows[:, :, None], spectra, jnp.zeros_like(spectra))
    spread = lax.all_to_all(masked, "af", split_axis=1, concat_axis=2, tiled=True)
    fourier = lax.psum_scatter(
        jnp.einsum("sjc,sjl->cls", spread, legendre, preferred_element_type=jnp.float32),
        "af",
        scatter_dimension=0,
        tiled=True,
    )
    fourier = fourier.astype(jnp.bfloat16)
    flattened = fourier.reshape(group_cols, lat_count * slot_count)
    arrived = lax.all_to_all(flattened, "wa", split_axis=1, concat_axis=1, tiled=True)
    coeffs = (
        arrived.reshape(group_cols, wa_count, lat_rows, slot_count)
        .transpose(0, 2, 1, 3)
        .reshape(group_cols, lat_rows, total_waves)
    )
    first_lon = lax.axis_index("af") * lon_count
    gathered = lax.all_gather(coeffs, "af", axis=0, tiled=True)
    halves = gathered.reshape(af_count, 2, group_fields, lat_rows, total_waves)
    real_part = halves[:, 0].reshape(af_count * group_fields, lat_rows, total_waves)
    imag_part = halves[:, 1].reshape(af_count * group_fields, lat_rows, total_waves)
    grid_fields, layer_out, demand_part, avail_part, partial_value = column_pass(
        real_part,
        imag_part,
        row_points,
        row_weight,
        wave_of_slot,
        first_lon,
        soil_water,
        land_mask,
        soil_type,
        plant_type,
        soil_params,
        root_profile,
    )
    partial_value = partial_value.reshape(lat_rows, 2 * FLUXES, total_waves)
    first_rows = jnp.arange(2 * FLUXES) < 2
    totals = lax.psum((demand_part, avail_part), ("wa", "af"))
    fix_ratio = UPTAKE_SHARE * totals[1] / totals[0]
    summed = sum_rows(partial_value * jnp.where(first_rows, fix_ratio, 1.0)[None, :, None])
    scaled = summed / jnp.sqrt(row_points.astype(jnp.float32))[:, None, None]
    weighted = (row_weight[:, None, None] * scaled).astype(jnp.bfloat16)
    returned = lax.all_to_all(weighted, "wa", split_axis=2, concat_axis=0, tiled=True)
    spectral = jnp.einsum("sjl,lqs->sqj", legendre, returned, preferred_element_type=jnp.float32)
    n_local = legendre.shape[1]
    global_rows = lax.axis_index("af") * n_local + jnp.arange(n_local, dtype=jnp.int32)
    kept_out = global_rows[None, :] < (total_waves - my_waves)[:, None]
    spectral = jnp.where(kept_out[:, None, :], spectral, 0.0)
    uptake = fix_ratio * layer_out
    return (grid_fields, uptake, spectral)


def solution(mesh):
    in_specs = (
        P("wa", None, "af"),
        P("wa", "af", None),
        P(),
        P("wa"),
        P("wa"),
        P("wa", None, "af"),
        P("wa", "af"),
        P("wa", "af"),
        P("wa", "af"),
        P(),
        P(),
    )
    out_specs = (P("wa", None, "af"), P("wa", None, "af"), P("wa", None, "af"))
    return jax.shard_map(
        per_device, mesh=mesh, in_specs=in_specs, out_specs=out_specs, check_vma=False
    )
```

profile of v0, /device:TPU:0, one launch (start us, length us, event | category | flops | bytes accessed | tf_op | source)
XLA Modules:
  0.0 186.7 jit_solution(5181856369862252046)
XLA Ops:
  7.9 1.2 copy.29
  9.4 0.9 reshape.1333
  10.2 4.2 %all-to-all-start = ((bf16[4,2,3200]{2,1,0:T(2,128)(2,1)}), bf16[4,2,3200]{2,1,0:T(2,128)(2,1)S(1)}, u32[]{:S(2)}, u32[]{:S(2)}) async-start(bf16[4,2,3200]{2,1,0:T(2,128)(2,1)} %reshape.1333), calls=%async_computation | async-start | bytes 102400 | tf_op jit(solution)/shard_map/all_to_all | solution.py:201
  14.5 4.0 %all-to-all-done = bf16[4,2,3200]{2,1,0:T(2,128)(2,1)S(1)} async-done(((bf16[4,2,3200]{2,1,0:T(2,128)(2,1)}), bf16[4,2,3200]{2,1,0:T(2,128)(2,1)S(1)}, u32[]{:S(2)}, u32[]{:S(2)}) %all-to-all-start) | async-done | bytes 51232 | tf_op jit(solution)/shard_map/all_to_all | solution.py:201
  19.7 0.9 reshape.1331
  20.7 20.3 %reduce-scatter.4.cloned.1.call-done = f32[32,80]{1,0:T(8,128)} async-done(((f32[128,80]{1,0:T(8,128)}), f32[32,80]{1,0:T(8,128)}) %reduce-scatter.4.cloned.1.call-update) | async-done | bytes 10256
  41.0 0.9 reshape.1332
  42.0 0.7 reshape.1335
  42.7 5.5 %all-to-all-start.1 = ((bf16[8,2,160]{2,1,0:T(2,128)(2,1)}), bf16[8,2,160]{2,1,0:T(2,128)(2,1)S(1)}, u32[]{:S(2)}, u32[]{:S(2)}) async-start(bf16[8,2,160]{2,1,0:T(2,128)(2,1)} %reshape.1335), calls=%async_computation.1 | async-start | bytes 16384 | tf_op jit(solution)/shard_map/all_to_all | solution.py:210
  49.7 0.7 copy-done.2
  50.4 4.3 %all-to-all-done.1 = bf16[8,2,160]{2,1,0:T(2,128)(2,1)S(1)} async-done(((bf16[8,2,160]{2,1,0:T(2,128)(2,1)}), bf16[8,2,160]{2,1,0:T(2,128)(2,1)S(1)}, u32[]{:S(2)}, u32[]{:S(2)}) %all-to-all-start.1) | async-done | bytes 5152 | tf_op jit(solution)/shard_map/all_to_all | solution.py:210
  54.9 5.2 %all_gather.3 = bf16[128,1,80]{2,0,1:T(8,128)(2,1)S(1)} all-gather(bf16[32,1,80]{2,0,1:T(8,128)(2,1)S(1)} %copy.33), channel_id=1, replica_groups=mesh['wa'=8,'af'=4] {'af'}, dimensions={0}, use_global_device_ids=true | all-gather | bytes 25600 | tf_op jit(solution)/shard_map/all_gather | solution.py:217
  60.2 0.7 copy-done.3
  60.8 59.2 %while.24 = (s32[]{:T(128)}, bf16[1,64,1280]{2,1,0:T(8,128)(2,1)S(1)}, f32[1,4,1280]{2,1,0:T(4,128)S(1)}, f32[]{:T(128)}, f32[]{:T(128)}, /*index=5*/f32[1,4,2,8...) while((s32[]{:T(128)}, ...), condition=%wide.region_11.12_spmd.clone, body=%wide.region_2.11_spmd.clone.sunk | while | flops 8385051 | bytes 354533 | solution.py:168
  61.5 1.3 fusion.76
  62.8 1.3 fusion.77
  64.1 0.7 fusion.79
  64.8 0.7 slice_multiply_fusion.3
  65.4 0.7 constant_dynamic-slice_fusion.8
  66.5 2.2 %multiply_reduce_fusion.3 = (f32[]{:T(128)}, f32[1,256]{1,0:T(1,128)S(1)}, f32[1,256]{1,0:T(1,128)S(1)}, f32[1,256]{1,0:T(1,128)S(1)}, f32[1,256]{1,0:T(1,128)S(...) fusion(f32[]{:T(128)} %bitcast.169, f32[1,256]{1,0:T(1,128)S(1)} %bitcast.188, ...), kind=kLoop, calls=%fused_computation.74.clone.1 | loop fusion | flops 14078 | bytes 20516 | tf_op jit(solution)/shard_map/while/body/eval_jaxpr/reduce_sum | solution.py:142
  68.6 1.3 convolution_bitcast_fusion.3
  70.0 1.4 fusion.80
  72.7 0.7 broadcast_compare_fusion.3
  73.3 1.3 fusion.76
  74.6 1.3 fusion.77
  75.9 0.7 fusion.79
  76.6 0.7 slice_multiply_fusion.3
  77.3 0.7 constant_dynamic-slice_fusion.8
  78.3 2.2 %multiply_reduce_fusion.3 = (f32[]{:T(128)}, f32[1,256]{1,0:T(1,128)S(1)}, f32[1,256]{1,0:T(1,128)S(1)}, f32[1,256]{1,0:T(1,128)S(1)}, f32[1,256]{1,0:T(1,128)S(...) fusion(f32[]{:T(128)} %bitcast.169, f32[1,256]{1,0:T(1,128)S(1)} %bitcast.188, ...), kind=kLoop, calls=%fused_computation.74.clone.1 | loop fusion | flops 14078 | bytes 20516 | tf_op jit(solution)/shard_map/while/body/eval_jaxpr/reduce_sum | solution.py:142
  80.5 1.3 convolution_bitcast_fusion.3
  81.8 1.4 fusion.80
  84.5 0.7 broadcast_compare_fusion.3
  85.2 1.3 fusion.76
  86.5 1.3 fusion.77
  87.8 0.7 fusion.79
  88.5 0.7 slice_multiply_fusion.3
  89.1 0.7 constant_dynamic-slice_fusion.8
  90.1 2.2 %multiply_reduce_fusion.3 = (f32[]{:T(128)}, f32[1,256]{1,0:T(1,128)S(1)}, f32[1,256]{1,0:T(1,128)S(1)}, f32[1,256]{1,0:T(1,128)S(1)}, f32[1,256]{1,0:T(1,128)S(...) fusion(f32[]{:T(128)} %bitcast.169, f32[1,256]{1,0:T(1,128)S(1)} %bitcast.188, ...), kind=kLoop, calls=%fused_computation.74.clone.1 | loop fusion | flops 14078 | bytes 20516 | tf_op jit(solution)/shard_map/while/body/eval_jaxpr/reduce_sum | solution.py:142
  92.3 1.3 convolution_bitcast_fusion.3
  93.6 1.4 fusion.80
  96.3 0.7 broadcast_compare_fusion.3
  97.0 1.3 fusion.76
  98.3 1.3 fusion.77
  99.6 0.7 fusion.79
  100.3 0.7 slice_multiply_fusion.3
  101.0 0.7 constant_dynamic-slice_fusion.8
  102.0 2.2 %multiply_reduce_fusion.3 = (f32[]{:T(128)}, f32[1,256]{1,0:T(1,128)S(1)}, f32[1,256]{1,0:T(1,128)S(1)}, f32[1,256]{1,0:T(1,128)S(1)}, f32[1,256]{1,0:T(1,128)S(...) fusion(f32[]{:T(128)} %bitcast.169, f32[1,256]{1,0:T(1,128)S(1)} %bitcast.188, ...), kind=kLoop, calls=%fused_computation.74.clone.1 | loop fusion | flops 14078 | bytes 20516 | tf_op jit(solution)/shard_map/while/body/eval_jaxpr/reduce_sum | solution.py:142
  104.2 1.3 convolution_bitcast_fusion.3
  105.5 1.4 fusion.80
  108.2 0.7 broadcast_compare_fusion.3
  108.8 1.3 fusion.76
  110.1 1.3 fusion.77
  111.5 0.7 fusion.79
  112.1 0.7 slice_multiply_fusion.3
  112.8 0.7 constant_dynamic-slice_fusion.8
  113.8 2.2 %multiply_reduce_fusion.3 = (f32[]{:T(128)}, f32[1,256]{1,0:T(1,128)S(1)}, f32[1,256]{1,0:T(1,128)S(1)}, f32[1,256]{1,0:T(1,128)S(1)}, f32[1,256]{1,0:T(1,128)S(...) fusion(f32[]{:T(128)} %bitcast.169, f32[1,256]{1,0:T(1,128)S(1)} %bitcast.188, ...), kind=kLoop, calls=%fused_computation.74.clone.1 | loop fusion | flops 14078 | bytes 20516 | tf_op jit(solution)/shard_map/while/body/eval_jaxpr/reduce_sum | solution.py:142
  116.0 1.3 convolution_bitcast_fusion.3
  117.3 1.4 fusion.80
  120.0 39.6 %all-reduce = (f32[]{:T(128)}, f32[]{:T(128)}) all-reduce(f32[]{:T(128)} %get-tuple-element.430, f32[]{:T(128)} %get-tuple-element.431), channel_id=1, replica_groups=mesh['wa'=8,'af'=4] {'wa','af'}, use_global_device_ids=true, to_apply=%region_12.13 | all-reduce | flops 2 | bytes 16 | tf_op jit(solution)/shard_map/psum | solution.py:237
  161.0 6.0 %psum.23 = f32[1,8,80]{2,1,0:T(8,128)S(1)} all-reduce(f32[1,8,80]{2,1,0:T(8,128)S(1)} %broadcast_multiply_fusion.1), channel_id=1, replica_groups=mesh['wa'=8,'af'=4] {'af'}, use_global_device_ids=true, to_apply=%region_14.15 | all-reduce | flops 640 | bytes 5120 | tf_op jit(solution)/shard_map/psum | solution.py:172
  167.0 0.7 copy.35
  167.8 4.3 %all-to-all-start.2 = ((bf16[1,8,80]{1,0,2:T(2,128)(2,1)}), bf16[1,8,80]{1,0,2:T(2,128)(2,1)S(1)}, u32[]{:S(2)}, u32[]{:S(2)}) async-start(bf16[1,8,80]{1,0,2:T(2,128)(2,1)} %copy.35), calls=%async_computation.2 | async-start | bytes 81920 | tf_op jit(solution)/shard_map/all_to_all | solution.py:242
  172.7 6.1 %all-to-all-done.2 = bf16[1,8,80]{1,0,2:T(2,128)(2,1)S(1)} async-done(((bf16[1,8,80]{1,0,2:T(2,128)(2,1)}), bf16[1,8,80]{1,0,2:T(2,128)(2,1)S(1)}, u32[]{:S(2)}, u32[]{:S(2)}) %all-to-all-start.2) | async-done | bytes 1312 | tf_op jit(solution)/shard_map/all_to_all | solution.py:242
  179.1 0.8 convolution_select_fusion
  (94 shorter events, 6.2 us)
Async XLA Ops:
  7.2 11.9 %copy-start = (bf16[10,20,8]{1,2,0:T(8,128)(2,1)S(1)}, bf16[10,20,8]{1,2,0:T(8,128)(2,1)}, u32[]{:S(2)}) copy-start(bf16[10,20,8]{1,2,0:T(8,128)(2,1)} %param.14) | copy-start | bytes 9604
  7.2 0.7 copy-start.4
  10.2 8.3 %all-to-all-start = ((bf16[4,2,3200]{2,1,0:T(2,128)(2,1)}), bf16[4,2,3200]{2,1,0:T(2,128)(2,1)S(1)}, u32[]{:S(2)}, u32[]{:S(2)}) async-start(bf16[4,2,3200]{2,1,0:T(2,128)(2,1)} %reshape.1333), calls=%async_computation | async-start | bytes 102400 | tf_op jit(solution)/shard_map/all_to_all | solution.py:201
  14.5 26.5 %reduce-scatter.4.cloned.1.call-start = ((), (), s32[]{:S(2)}) async-start(), calls=%async_computation.4 | async-start | bytes 81920
  42.7 12.0 %all-to-all-start.1 = ((bf16[8,2,160]{2,1,0:T(2,128)(2,1)}), bf16[8,2,160]{2,1,0:T(2,128)(2,1)S(1)}, u32[]{:S(2)}, u32[]{:S(2)}) async-start(bf16[8,2,160]{2,1,0:T(2,128)(2,1)} %reshape.1335), calls=%async_computation.1 | async-start | bytes 16384 | tf_op jit(solution)/shard_map/all_to_all | solution.py:210
  49.7 0.7 copy-start.2
  60.1 0.7 copy-start.3
  120.0 59.9 %copy-start.1 = (bf16[1,64,1280]{2,1,0:T(8,128)(2,1)}, bf16[1,64,1280]{2,1,0:T(8,128)(2,1)S(1)}, u32[]{:S(2)}) copy-start(bf16[1,64,1280]{2,1,0:T(8,128)(2,1)S(1)} %get-tuple-element.426) | copy-start | bytes 491524
  167.8 11.1 %all-to-all-start.2 = ((bf16[1,8,80]{1,0,2:T(2,128)(2,1)}), bf16[1,8,80]{1,0,2:T(2,128)(2,1)S(1)}, u32[]{:S(2)}, u32[]{:S(2)}) async-start(bf16[1,8,80]{1,0,2:T(2,128)(2,1)} %copy.35), calls=%async_computation.2 | async-start | bytes 81920 | tf_op jit(solution)/shard_map/all_to_all | solution.py:242
Sparse Core Ops, SparseCore 0:
  20.8 20.1 reduce-scatter.3
where the time goes:
time: 188 us; the launch traced here: 187 us
  blocking collectives  50.8 us (27%)
  waiting for transfers between devices  34.9 us (19%)
  matrix products  27.4 us (15%)
  other arithmetic  23.7 us (13%)
  between operations  16.9 us (9%)
  starting transfers between devices  14.1 us (8%)
  local copies, waits for them, and re-layouts  12.5 us (7%)
  loops' own time  6.5 us (3%)
    psum x1, blocking collectives, per_device(): totals = lax.psum((demand_part, avail_part), ('wa', 'af'))  39.6 us
    unnamed x2, waiting for transfers between devices  20.4 us
    reduce_sum x5, other arithmetic, one_block(): demand_part = demand_part + jnp.sum(cell_area * transpiration)  10.9 us
    unnamed x19, local copies, waits for them, and re-layouts  7.45 us
    dot_general x5, matrix products, one_block(): jnp.einsum('rql,rml->rqm', values, sine_table, precision=lax.Precision.HI...  6.86 us
    dot_general x5, matrix products, one_block(): jnp.einsum('rql,rml->rqm', values, cosine_table, precision=lax.Precision....  6.62 us
    dot_general x5, matrix products, synth_block(): jnp.einsum('frm,rml->rfl', imag_part, sine_table, preferred_element_type=...  6.59 us
    another operation x1, loops' own time, column_pass(): return lax.fori_loop(0, lon_count // lon_block, one_block, start)  6.5 us
  transfers between devices with their start and end apart: 4, of which 4 were waited for; matrix products, arithmetic and copies ran while one was open for 0% of the time, Pallas kernels for 0%

commit v1 on v0

v1 whole, which is shorter than its diff:
```python
import functools
import math

import jax
import jax.numpy as jnp
from jax import lax
from jax.experimental import pallas as pl
from jax.experimental.pallas import tpu as pltpu
from jax.sharding import PartitionSpec as P

LEVELS = 8
FLUXES = 4
SOIL_LAYERS = 4
TWO_PI = 2.0 * math.pi
DEPTHS = (0.07, 0.21, 0.72, 1.89)
UPTAKE_SHARE = 4.0
MESH = pl.DeviceIdType.MESH
HIGHEST = lax.Precision.HIGHEST
SLOT_PAD = 16
CHUNK_WA = 8
CHUNK = SLOT_PAD * CHUNK_WA
LANES = 128


def dot(lhs, rhs, lhs_dim, rhs_dim, precision=None):
    return lax.dot_general(
        lhs,
        rhs,
        (((lhs_dim,), (rhs_dim,)), ((), ())),
        precision=precision,
        preferred_element_type=jnp.float32,
    )


def iota(shape, dim):
    return lax.broadcasted_iota(jnp.int32, shape, dim)


def cos_sin(waves, longitudes, points):
    product = waves * longitudes
    residue = product - points * jnp.round(product * (1.0 / points))
    angle = residue * (TWO_PI / points)
    return jnp.cos(angle), jnp.sin(angle)


def kernel(
    wa_count,
    af_count,
    spectra_ref,
    legendre_ref,
    wave_smem,
    wave_ref,
    points_smem,
    weight_smem,
    water_ref,
    land_ref,
    soil_ref,
    plant_ref,
    params_ref,
    roots_ref,
    grid_ref,
    uptake_ref,
    spectral_ref,
    leg_all,
    placed,
    four_rows,
    four_send,
    four_recv,
    tables,
    coef_send,
    coef_recv,
    send_sems,
    recv_sems,
):
    slots, offsets, cols = spectra_ref.shape
    n_local = legendre_ref.shape[1]
    lat_count = legendre_ref.shape[2]
    waves_total = wave_ref.shape[1]
    lon_count = water_ref.shape[2]
    group = cols // 2
    devices = wa_count * af_count
    chunks = wa_count // CHUNK_WA
    my_wa = lax.axis_index("wa")
    my_af = lax.axis_index("af")
    me = my_wa * af_count + my_af
    my_block = my_af * wa_count + my_wa

    def partner(step):
        other = lax.rem(me + step, devices)
        return lax.div(other, af_count), lax.rem(other, af_count)

    barrier = pltpu.get_barrier_semaphore()

    def greet(step, carry):
        pl.semaphore_signal(barrier, inc=1, device_id=partner(step), device_id_type=MESH)
        return carry

    lax.fori_loop(1, devices, greet, 0)

    place = (
        iota((n_local, offsets), 1) == iota((n_local, offsets), 0) + my_af * n_local
    ).astype(jnp.float32).astype(jnp.bfloat16)
    lane_offset = iota((lat_count, offsets), 1)
    parts = []
    for s in range(slots):
        turned = dot(legendre_ref[s], place, 0, 0)
        kept = lane_offset < waves_total - wave_smem[my_wa * slots + s]
        parts.append(jnp.where(kept, turned, 0.0))
    leg_all[my_af] = jnp.concatenate(parts, axis=0).astype(jnp.bfloat16)

    pl.semaphore_wait(barrier, devices - 1)

    def send_legendre(step, carry):
        pltpu.make_async_remote_copy(
            src_ref=leg_all.at[my_af],
            dst_ref=leg_all.at[my_af],
            send_sem=send_sems.at[0],
            recv_sem=recv_sems.at[0],
            device_id=(my_wa, lax.rem(my_af + step, af_count)),
            device_id_type=MESH,
        ).start()
        return carry

    lax.fori_loop(1, af_count, send_legendre, 0)

    col_place = (
        iota((cols, LANES), 1) == iota((cols, LANES), 0) + my_af * cols
    ).astype(jnp.float32).astype(jnp.bfloat16)
    for s in range(slots):
        placed[s] = dot(spectra_ref[s], col_place, 1, 0).astype(jnp.bfloat16)
    four_rows[...] = jnp.zeros_like(four_rows)

    leg_bytes = leg_all.at[pl.ds(0, af_count - 1)]
    pltpu.make_async_copy(leg_bytes, leg_bytes, recv_sems.at[0]).wait()

    for s in range(slots):
        rows = pl.ds(s * lat_count, lat_count)
        full = leg_all[0, rows, :].astype(jnp.float32)
        for other in range(1, af_count):
            full = full + leg_all[other, rows, :].astype(jnp.float32)
        four_rows[pl.ds(s, lat_count, stride=SLOT_PAD), :] = dot(
            full.astype(jnp.bfloat16), placed[s], 1, 0
        )
    four_send[...] = four_rows[...].astype(jnp.bfloat16).reshape(four_send.shape)

    def send_fourier(step, carry):
        to_wa, to_af = partner(step)
        pltpu.make_async_remote_copy(
            src_ref=four_send.at[to_wa],
            dst_ref=four_recv.at[my_block],
            send_sem=send_sems.at[1],
            recv_sem=recv_sems.at[1],
            device_id=(to_wa, to_af),
            device_id_type=MESH,
        ).start()
        return carry

    lax.fori_loop(1, devices, send_fourier, 0)
    four_recv[my_block] = four_send[my_wa]

    points_int = points_smem[0]
    points = points_int.astype(jnp.float32)
    points_vec = jnp.full((1, 1), points, jnp.float32)
    first_lon = my_af * lon_count
    waves_row = wave_ref[...].astype(jnp.float32)

    def fill_tables(chunk, carry):
        row = iota((CHUNK, waves_total), 0)
        slot = lax.rem(row, SLOT_PAD)
        named = iota((CHUNK, waves_total), 1) == (
            (lax.div(row, SLOT_PAD) + chunk * CHUNK_WA) * slots + slot
        )
        named = jnp.logical_and(named, slot < slots)
        waves = jnp.sum(jnp.where(named, waves_row, 0.0), axis=1, keepdims=True)
        lane = iota((1, LANES), 1)
        base_cos, base_sin = cos_sin(waves, lane.astype(jnp.float32), points_vec)
        starts = (first_lon + LANES * lane).astype(jnp.float32)
        start_cos, start_sin = cos_sin(waves, starts, points_vec)
        for block in range(lon_count // LANES):
            part = pl.ds(block * LANES, LANES)
            c0 = start_cos[:, block : block + 1]
            s0 = start_sin[:, block : block + 1]
            tables[chunk, pl.ds(0, CHUNK), part] = (base_cos * c0 - base_sin * s0).astype(
                jnp.bfloat16
            )
            tables[chunk, pl.ds(CHUNK, CHUNK), part] = (
                -(base_sin * c0) - base_cos * s0
            ).astype(jnp.bfloat16)
        return carry

    if chunks == 1:
        fill_tables(0, 0)
    else:
        lax.fori_loop(0, chunks, fill_tables, 0)

    longitudes = first_lon + iota((1, lon_count), 1)
    in_row = (longitudes < points_int).astype(jnp.float32)
    usable = in_row * land_ref[...].astype(jnp.float32)
    soil_kinds = params_ref.shape[1]
    plant_kinds = roots_ref.shape[0]
    soil_hot = (iota((soil_kinds, lon_count), 0) == soil_ref[...]).astype(jnp.float32)
    plant_hot = (iota((plant_kinds, lon_count), 0) == plant_ref[...]).astype(jnp.float32)
    soil = dot(params_ref[...], soil_hot, 1, 0, HIGHEST)
    wilting = 0.04 + 0.1 * soil[0:1]
    capacity = 0.3 + 0.15 * soil[1:2]
    roots = roots_ref[...]
    fractions = roots / jnp.sum(roots, axis=1, keepdims=True)
    root_share = dot(fractions, plant_hot, 0, 0, HIGHEST)
    moisture = water_ref[0]
    excess = moisture - wilting
    factor = jnp.clip(excess / (capacity - wilting), 0.0, 1.0)
    share_factor = root_share * factor
    stress = jnp.sum(share_factor, axis=0, keepdims=True)
    layer = iota((SOIL_LAYERS, 1), 0)
    depths = jnp.full((SOIL_LAYERS, 1), DEPTHS[0], jnp.float32)
    for number in range(1, SOIL_LAYERS):
        depths = jnp.where(layer == number, DEPTHS[number], depths)
    reserve = jnp.sum(root_share * depths * jnp.maximum(excess, 0.0), axis=0, keepdims=True)
    available = usable * reserve

    four_bytes = four_recv.at[pl.ds(0, devices - 1)]
    pltpu.make_async_copy(four_bytes, four_bytes, recv_sems.at[1]).wait()

    def synthesize(chunk, total):
        summed = jnp.zeros((CHUNK, LANES), jnp.float32)
        for other in range(af_count):
            got = four_recv[pl.ds(other * wa_count + chunk * CHUNK_WA, CHUNK_WA)]
            summed = summed + got.reshape(CHUNK, LANES).astype(jnp.float32)
        turned = summed.T
        real = [turned[cols * g : cols * g + group] for g in range(af_count)]
        imag = [turned[cols * g + group : cols * (g + 1)] for g in range(af_count)]
        both = jnp.concatenate(
            [jnp.concatenate(real, axis=0), jnp.concatenate(imag, axis=0)], axis=1
        ).astype(jnp.bfloat16)
        return total + dot(both, tables[chunk], 1, 0)

    fields = jnp.zeros((group * af_count, lon_count), jnp.float32)
    if chunks == 1:
        fields = synthesize(0, fields)
    else:
        fields = lax.fori_loop(0, chunks, synthesize, fields)
    rounded = (fields * in_row * (1.0 / math.sqrt(waves_total))).astype(jnp.bfloat16)
    grid_ref[0] = rounded
    values = rounded.astype(jnp.float32)

    def lowest(field):
        return values[(field + 1) * LEVELS - 1 : (field + 1) * LEVELS]

    wind_u, wind_v, air, humid, skin = [lowest(f) for f in range(5)]
    speed = jnp.sqrt(1.0 + wind_u * wind_u + wind_v * wind_v)
    gap = air - humid
    softplus = jnp.maximum(gap, 0.0) + jnp.log1p(jnp.exp(-jnp.abs(gap)))
    demand = usable * (0.5 * speed * softplus)
    transpiration = demand * stress
    moving = in_row * speed
    fluxes = (transpiration, moving * (skin - air), moving * wind_u, moving * wind_v)
    nothing = jnp.zeros_like(demand)
    even, odd = [], []
    for flux in fluxes:
        even += [flux, nothing]
        odd += [nothing, flux]
    even = jnp.concatenate(even, axis=0)
    odd = jnp.concatenate(odd, axis=0)
    even = jnp.concatenate([even] * SLOT_PAD, axis=0).astype(jnp.bfloat16)
    odd = jnp.concatenate([odd] * SLOT_PAD, axis=0).astype(jnp.bfloat16)
    weight = weight_smem[0]
    area = weight / points_vec
    transpired = jnp.sum(transpiration, axis=1, keepdims=True) * area
    reserved = jnp.sum(available, axis=1, keepdims=True) * area
    row_scale = weight * lax.rsqrt(points_vec)

    rows8 = 2 * FLUXES
    first_spare = slots * rows8

    def analyse(chunk, carry):
        product = dot(tables[chunk, pl.ds(0, CHUNK), :], even, 1, 1) + dot(
            tables[chunk, pl.ds(CHUNK, CHUNK), :], odd, 1, 1
        )
        slot = lax.rem(iota((CHUNK, LANES), 0), SLOT_PAD)
        lane = iota((CHUNK, LANES), 1)
        mine = jnp.logical_and(lax.div(lane, rows8) == slot, slot < slots)
        kept = jnp.where(mine, product, 0.0).reshape(CHUNK_WA, SLOT_PAD, LANES)
        line = jnp.sum(kept, axis=1) * row_scale
        lane = iota((CHUNK_WA, LANES), 1)
        line = jnp.where(lane == first_spare, transpired, line)
        line = jnp.where(lane == first_spare + 1, reserved, line)
        coef_send[pl.ds(chunk * CHUNK_WA, CHUNK_WA)] = line.reshape(CHUNK_WA, 1, LANES)
        return carry

    if chunks == 1:
        analyse(0, 0)
    else:
        lax.fori_loop(0, chunks, analyse, 0)

    def send_coeffs(step, carry):
        to_wa, to_af = partner(step)
        pltpu.make_async_remote_copy(
            src_ref=coef_send.at[to_wa],
            dst_ref=coef_recv.at[my_block],
            send_sem=send_sems.at[2],
            recv_sem=recv_sems.at[2],
            device_id=(to_wa, to_af),
            device_id_type=MESH,
        ).start()
        return carry

    lax.fori_loop(1, devices, send_coeffs, 0)
    coef_recv[my_block] = coef_send[my_wa]
    unfixed = demand * share_factor
    pltpu.make_async_copy(leg_bytes, leg_bytes, send_sems.at[0]).wait()
    pltpu.make_async_copy(four_bytes, four_bytes, send_sems.at[1]).wait()

    coef_bytes = coef_recv.at[pl.ds(0, devices - 1)]
    pltpu.make_async_copy(coef_bytes, coef_bytes, recv_sems.at[2]).wait()

    lines = coef_recv[pl.ds(0, wa_count)]
    for other in range(1, af_count):
        lines = lines + coef_recv[pl.ds(other * wa_count, wa_count)]
    lines = lines.reshape(wa_count, LANES)
    totals = jnp.sum(lines, axis=0, keepdims=True)
    fix_ratio = UPTAKE_SHARE * totals[:, first_spare + 1 : first_spare + 2] / (
        totals[:, first_spare : first_spare + 1]
    )
    uptake_ref[0] = fix_ratio * unfixed
    scaled = jnp.where(lax.rem(iota((1, LANES), 1), rows8) < 2, fix_ratio, 1.0) * lines
    turned = scaled.T
    offset = iota((rows8, n_local), 1) + my_af * n_local
    for s in range(slots):
        weighted = turned[s * rows8 : (s + 1) * rows8].astype(jnp.bfloat16)
        result = dot(weighted, legendre_ref[s], 1, 1)
        kept = offset < waves_total - wave_smem[my_wa * slots + s]
        spectral_ref[s] = jnp.where(kept, result, 0.0)

    pltpu.make_async_copy(coef_bytes, coef_bytes, send_sems.at[2]).wait()


def per_device(
    spectra,
    legendre,
    wave_of_slot,
    row_points,
    row_weight,
    soil_water,
    land_mask,
    soil_type,
    plant_type,
    soil_params,
    root_profile,
):
    wa_count = lax.axis_size("wa")
    af_count = lax.axis_size("af")
    slots, offsets, cols = spectra.shape
    n_local, lat_count = legendre.shape[1:]
    waves_total = wave_of_slot.shape[0]
    lon_count = soil_water.shape[2]
    devices = wa_count * af_count
    chunks = wa_count // CHUNK_WA
    assert row_points.shape[0] == 1 and lat_count == wa_count and cols * af_count == LANES
    assert slots * 2 * FLUXES + 2 <= LANES and slots <= SLOT_PAD
    assert wa_count % CHUNK_WA == 0 and lon_count % LANES == 0
    vmem = pl.BlockSpec(memory_space=pltpu.VMEM)
    smem = pl.BlockSpec(memory_space=pltpu.SMEM)
    return pl.pallas_call(
        functools.partial(kernel, wa_count, af_count),
        out_shape=(
            jax.ShapeDtypeStruct((1, cols // 2 * af_count, lon_count), jnp.bfloat16),
            jax.ShapeDtypeStruct((1, SOIL_LAYERS, lon_count), jnp.float32),
            jax.ShapeDtypeStruct((slots, 2 * FLUXES, n_local), jnp.float32),
        ),
        in_specs=[vmem, vmem, smem, vmem, smem, smem] + [vmem] * 6,
        out_specs=(vmem, vmem, vmem),
        scratch_shapes=[
            pltpu.VMEM((af_count, slots * lat_count, offsets), jnp.bfloat16),
            pltpu.VMEM((slots, offsets, LANES), jnp.bfloat16),
            pltpu.VMEM((lat_count * SLOT_PAD, LANES), jnp.float32),
            pltpu.VMEM((lat_count, SLOT_PAD, LANES), jnp.bfloat16),
            pltpu.VMEM((devices, SLOT_PAD, LANES), jnp.bfloat16),
            pltpu.VMEM((chunks, 2 * CHUNK, lon_count), jnp.bfloat16),
            pltpu.VMEM((wa_count, 1, LANES), jnp.float32),
            pltpu.VMEM((devices, 1, LANES), jnp.float32),
            pltpu.SemaphoreType.DMA((3,)),
            pltpu.SemaphoreType.DMA((3,)),
        ],
        compiler_params=pltpu.CompilerParams(
            collective_id=0,
            has_side_effects=True,
            vmem_limit_bytes=(48 if chunks > 1 else 16) * 1024 * 1024,
        ),
    )(
        spectra,
        legendre,
        wave_of_slot,
        wave_of_slot.reshape(1, waves_total),
        row_points,
        row_weight,
        soil_water,
        land_mask,
        soil_type,
        plant_type,
        soil_params,
        root_profile,
    )


def solution(mesh):
    in_specs = (
        P("wa", None, "af"),
        P("wa", "af", None),
        P(),
        P("wa"),
        P("wa"),
        P("wa", None, "af"),
        P("wa", "af"),
        P("wa", "af"),
        P("wa", "af"),
        P(),
        P(),
    )
    out_specs = (P("wa", None, "af"), P("wa", None, "af"), P("wa", None, "af"))
    return jax.shard_map(
        per_device, mesh=mesh, in_specs=in_specs, out_specs=out_specs, check_vma=False
    )
```

time: 188 us -> 28.3 us (0.15)
  blocking collectives: 50.8 us -> 0 us
  waiting for transfers between devices: 34.9 us -> 0 us
  matrix products: 27.4 us -> 0 us
  other arithmetic: 23.7 us -> 0 us
  Pallas kernels: 0 us -> 21.7 us
  between operations: 16.9 us -> 2.03 us
  starting transfers between devices: 14.1 us -> 0 us
  local copies, waits for them, and re-layouts: 12.5 us -> 4.25 us
  loops' own time: 6.5 us -> 0 us
    psum x2 -> x0, blocking collectives: 45.6 us -> none  [the longest x1 39.6 us: per_device(): totals = lax.psum((demand_part, avail_part), ('wa', 'af'))]
    dot_general x22 -> x0, matrix products: 27.4 us -> none  [the longest x5 6.86 us: one_block(): jnp.einsum('rql,rml->rqm', values, sine_table, precision=lax.Precision.HI...]
    pallas_call x0 -> x1, Pallas kernels: none -> 21.7 us  [per_device(): pl.pallas_call(functools.partial(kernel, wa_count, af_count), out_shape=(...]
    unnamed x2 -> x0, waiting for transfers between devices: 20.4 us -> none
    all_to_all x3 -> x0, waiting for transfers between devices: 14.5 us -> none  [the longest x1 6.13 us: per_device(): lax.all_to_all(weighted, 'wa', split_axis=2, concat_axis=0, tiled=True)]
    all_to_all x3 -> x0, starting transfers between devices: 14.1 us -> none  [the longest x1 5.51 us: per_device(): lax.all_to_all(flattened, 'wa', split_axis=1, concat_axis=1, tiled=True)]
    reduce_sum x16 -> x0, other arithmetic: 12.3 us -> none  [the longest x5 10.9 us: one_block(): demand_part = demand_part + jnp.sum(cell_area * transpiration)]
    mul x12 -> x0, other arithmetic: 7.25 us -> none  [the longest x5 3.3 us: physics(): in_row * wind_speed * (skin_temp - air_temp)]
  transfers between devices with their start and end apart: 4 -> 0, of which waited for: 4 -> 0; matrix products, arithmetic and copies ran while one was open for 0% -> 0% of each run, Pallas kernels for 0% -> 0%
where the time goes in v1:
time: 28.3 us; the launch traced here: 28 us
  Pallas kernels  21.7 us (77%)
  local copies, waits for them, and re-layouts  4.25 us (15%)
  between operations  2.03 us (7%)
    pallas_call x1, Pallas kernels, per_device(): pl.pallas_call(functools.partial(kernel, wa_count, af_count), out_shape=(...  21.7 us
    unnamed x20, local copies, waits for them, and re-layouts  4.25 us

profile of v1, /device:TPU:0, one launch (start us, length us, event | category | flops | bytes accessed | tf_op | source)
XLA Modules:
  0.0 28.0 jit_solution(586077694057085544)
XLA Ops:
  0.6 0.0 copy-start.6
  2.0 0.8 %copy.16.roots_ref = f32[20,4]{1,0:T(8,128)S(1)} copy(f32[20,4]{0,1:T(4,128)} %param.21) | data formatting | bytes 640 | tf_op args[10]
  2.7 0.9 %copy.15.legendre_ref = bf16[10,20,8]{2,1,0:T(8,128)(2,1)S(1)} copy(bf16[10,20,8]{1,2,0:T(8,128)(2,1)} %param.12) | data formatting | bytes 6400 | tf_op args[1]
  3.6 0.0 copy-done.6
  3.6 0.0 copy-start
  3.6 0.0 copy-start.1
  3.6 0.0 copy-start.2
  3.6 0.0 copy-start.3
  3.7 0.0 copy-start.4
  3.7 0.0 copy-start.5
  3.7 0.2 copy.14.spectra_ref
  3.8 0.5 %copy-done = f32[1,4,1280]{2,1,0:T(4,128)S(1)} copy-done((f32[1,4,1280]{2,1,0:T(4,128)S(1)}, f32[1,4,1280]{2,1,0:T(4,128)}, u32[]{:S(2)}) %copy-start) | copy-done | bytes 20504
  4.3 0.0 copy-done.1
  4.3 0.0 copy-done.2
  4.3 0.0 copy-done.3
  4.4 0.0 copy-done.4
  4.4 0.0 copy-done.5
  4.4 21.7 %shard_map.130 = (bf16[1,64,1280]{2,1,0:T(8,128)(2,1)S(1)}, f32[1,4,1280]{2,1,0:T(4,128)S(1)}, f32[10,8,20]{2,1,0:T(8,128)S(1)}) custom-call(bf16[10,80,32]{2,1,0:T(8,128)(2,1)S(1)} %copy.14.spectra_ref, bf16[10,20,8]{2,1,0:T(8,128)(2,1)S(1)} %copy.15.legendre_ref, s32[80]{0:T(128)S(1)} %copy-done.4, s32[1,80]{1,0:T(1,128)S(1)} %bitcast.1, ...), custom_call_target="tpu_custom_call" | custom-call | tf_op jit(solution)/shard_map/pallas_call | solution.py:363
  26.1 0.7 %copy.22 = bf16[1,64,1280]{2,1,0:T(8,128)(2,1)} copy(bf16[1,64,1280]{2,1,0:T(8,128)(2,1)S(1)} %get-tuple-element.6) | data formatting | bytes 327680
  26.8 0.6 %copy.23 = f32[1,4,1280]{2,1,0:T(4,128)} copy(f32[1,4,1280]{2,1,0:T(4,128)S(1)} %get-tuple-element.7) | data formatting | bytes 40960
  27.4 0.6 %copy.24 = f32[10,8,20]{2,1,0:T(8,128)} copy(f32[10,8,20]{2,1,0:T(8,128)S(1)} %get-tuple-element.8) | data formatting | bytes 12800
Async XLA Ops:
  0.6 3.0 %copy-start.6 = (bf16[10,80,32]{1,2,0:T(8,128)(2,1)S(1)}, bf16[10,80,32]{1,2,0:T(8,128)(2,1)}, u32[]{:S(2)}) copy-start(bf16[10,80,32]{1,2,0:T(8,128)(2,1)} %param.11) | copy-start | bytes 153604
  3.6 0.7 %copy-start = (f32[1,4,1280]{2,1,0:T(4,128)S(1)}, f32[1,4,1280]{2,1,0:T(4,128)}, u32[]{:S(2)}) copy-start(f32[1,4,1280]{2,1,0:T(4,128)} %water_ref.1) | copy-start | bytes 61444
  3.6 0.7 %copy-start.1 = (s32[1,1280]{1,0:T(1,128)S(1)}, s32[1,1280]{1,0:T(1,128)}, u32[]{:S(2)}) copy-start(s32[1,1280]{1,0:T(1,128)} %land_ref.1) | copy-start | bytes 15364
  3.6 0.7 %copy-start.2 = (s32[1,1280]{1,0:T(1,128)S(1)}, s32[1,1280]{1,0:T(1,128)}, u32[]{:S(2)}) copy-start(s32[1,1280]{1,0:T(1,128)} %soil_ref.1) | copy-start | bytes 15364
  3.6 0.7 %copy-start.3 = (s32[1,1280]{1,0:T(1,128)S(1)}, s32[1,1280]{1,0:T(1,128)}, u32[]{:S(2)}) copy-start(s32[1,1280]{1,0:T(1,128)} %plant_ref.1) | copy-start | bytes 15364
  3.7 0.7 %copy-start.4 = (s32[80]{0:T(128)S(1)}, s32[80]{0:T(128)}, u32[]{:S(2)}) copy-start(s32[80]{0:T(128)} %wave_smem.1) | copy-start | bytes 964
  3.7 0.7 %copy-start.5 = (f32[2,7]{1,0:T(2,128)S(1)}, f32[2,7]{1,0:T(2,128)}, u32[]{:S(2)}) copy-start(f32[2,7]{1,0:T(2,128)} %params_ref.1) | copy-start | bytes 172

commit v2 on v1

--- a/solution.py
+++ b/solution.py
@@ -39,8 +39,23 @@
 def cos_sin(waves, longitudes, points):
     product = waves * longitudes
     residue = product - points * jnp.round(product * (1.0 / points))
-    angle = residue * (TWO_PI / points)
-    return jnp.cos(angle), jnp.sin(angle)
+    quarters = residue * (4.0 / points)
+    quadrant = jnp.round(quarters)
+    angle = (quarters - quadrant) * (0.25 * TWO_PI)
+    square = angle * angle
+    cosine = 1.0 + square * (
+        -1 / 2 + square * (1 / 24 + square * (-1 / 720 + square * (1 / 40320)))
+    )
+    sine = angle * (
+        1.0 + square * (-1 / 6 + square * (1 / 120 + square * (-1 / 5040 + square * (1 / 362880))))
+    )
+    size = jnp.abs(quadrant)
+    odd = size == 1.0
+    sign = 1.0 - size
+    return (
+        jnp.where(odd, -quadrant * sine, sign * cosine),
+        jnp.where(odd, quadrant * cosine, sign * sine),
+    )
 
 
 def kernel(
@@ -72,9 +87,9 @@
     send_sems,
     recv_sems,
 ):
-    slots, offsets, cols = spectra_ref.shape
-    n_local = legendre_ref.shape[1]
-    lat_count = legendre_ref.shape[2]
+    slots, cols, offsets = spectra_ref.shape
+    lat_count = legendre_ref.shape[1]
+    n_local = legendre_ref.shape[2]
     waves_total = wave_ref.shape[1]
     lon_count = water_ref.shape[2]
     group = cols // 2
@@ -82,20 +97,30 @@
     chunks = wa_count // CHUNK_WA
     my_wa = lax.axis_index("wa")
     my_af = lax.axis_index("af")
-    me = my_wa * af_count + my_af
     my_block = my_af * wa_count + my_wa
 
-    def partner(step):
-        other = lax.rem(me + step, devices)
-        return lax.div(other, af_count), lax.rem(other, af_count)
+    def wrapped(index, count):
+        return jnp.where(index >= count, index - count, index)
+
+    af_peers = [my_af] + [wrapped(my_af + step, af_count) for step in range(1, af_count)]
+
+    def each_partner(act):
+        def row(step, carry):
+            to_wa = wrapped(my_wa + step, wa_count)
+            for to_af in af_peers:
+                act(to_wa, to_af)
+            return carry
+
+        lax.fori_loop(1, wa_count, row, 0)
+        for to_af in af_peers[1:]:
+            act(my_wa, to_af)
 
     barrier = pltpu.get_barrier_semaphore()
 
-    def greet(step, carry):
-        pl.semaphore_signal(barrier, inc=1, device_id=partner(step), device_id_type=MESH)
-        return carry
-
-    lax.fori_loop(1, devices, greet, 0)
+    def greet(to_wa, to_af):
+        pl.semaphore_signal(barrier, inc=1, device_id=(to_wa, to_af), device_id_type=MESH)
+
+    each_partner(greet)
 
     place = (
         iota((n_local, offsets), 1) == iota((n_local, offsets), 0) + my_af * n_local
@@ -103,60 +128,27 @@
     lane_offset = iota((lat_count, offsets), 1)
     parts = []
     for s in range(slots):
-        turned = dot(legendre_ref[s], place, 0, 0)
+        turned = dot(legendre_ref[s], place, 1, 0)
         kept = lane_offset < waves_total - wave_smem[my_wa * slots + s]
         parts.append(jnp.where(kept, turned, 0.0))
     leg_all[my_af] = jnp.concatenate(parts, axis=0).astype(jnp.bfloat16)
 
     pl.semaphore_wait(barrier, devices - 1)
 
-    def send_legendre(step, carry):
+    for to_af in af_peers[1:]:
         pltpu.make_async_remote_copy(
             src_ref=leg_all.at[my_af],
             dst_ref=leg_all.at[my_af],
             send_sem=send_sems.at[0],
             recv_sem=recv_sems.at[0],
-            device_id=(my_wa, lax.rem(my_af + step, af_count)),
+            device_id=(my_wa, to_af),
             device_id_type=MESH,
         ).start()
-        return carry
-
-    lax.fori_loop(1, af_count, send_legendre, 0)
-
-    col_place = (
-        iota((cols, LANES), 1) == iota((cols, LANES), 0) + my_af * cols
-    ).astype(jnp.float32).astype(jnp.bfloat16)
+
+    placed[...] = jnp.zeros_like(placed)
     for s in range(slots):
-        placed[s] = dot(spectra_ref[s], col_place, 1, 0).astype(jnp.bfloat16)
+        placed[s, pl.ds(pl.multiple_of(my_af * cols, cols), cols), :] = spectra_ref[s]
     four_rows[...] = jnp.zeros_like(four_rows)
-
-    leg_bytes = leg_all.at[pl.ds(0, af_count - 1)]
-    pltpu.make_async_copy(leg_bytes, leg_bytes, recv_sems.at[0]).wait()
-
-    for s in range(slots):
-        rows = pl.ds(s * lat_count, lat_count)
-        full = leg_all[0, rows, :].astype(jnp.float32)
-        for other in range(1, af_count):
-            full = full + leg_all[other, rows, :].astype(jnp.float32)
-        four_rows[pl.ds(s, lat_count, stride=SLOT_PAD), :] = dot(
-            full.astype(jnp.bfloat16), placed[s], 1, 0
-        )
-    four_send[...] = four_rows[...].astype(jnp.bfloat16).reshape(four_send.shape)
-
-    def send_fourier(step, carry):
-        to_wa, to_af = partner(step)
-        pltpu.make_async_remote_copy(
-            src_ref=four_send.at[to_wa],
-            dst_ref=four_recv.at[my_block],
-            send_sem=send_sems.at[1],
-            recv_sem=recv_sems.at[1],
-            device_id=(to_wa, to_af),
-            device_id_type=MESH,
-        ).start()
-        return carry
-
-    lax.fori_loop(1, devices, send_fourier, 0)
-    four_recv[my_block] = four_send[my_wa]
 
     points_int = points_smem[0]
     points = points_int.astype(jnp.float32)
@@ -193,19 +185,45 @@
     else:
         lax.fori_loop(0, chunks, fill_tables, 0)
 
+    leg_bytes = leg_all.at[pl.ds(0, af_count - 1)]
+    pltpu.make_async_copy(leg_bytes, leg_bytes, recv_sems.at[0]).wait()
+
+    for s in range(slots):
+        rows = pl.ds(s * lat_count, lat_count)
+        full = leg_all[0, rows, :].astype(jnp.float32)
+        for other in range(1, af_count):
+            full = full + leg_all[other, rows, :].astype(jnp.float32)
+        four_rows[pl.ds(s, lat_count, stride=SLOT_PAD), :] = dot(
+            full.astype(jnp.bfloat16), placed[s], 1, 1
+        )
+    four_send[...] = four_rows[...].astype(jnp.bfloat16).reshape(four_send.shape)
+
+    def send_fourier(to_wa, to_af):
+        pltpu.make_async_remote_copy(
+            src_ref=four_send.at[to_wa],
+            dst_ref=four_recv.at[my_block],
+            send_sem=send_sems.at[1],
+            recv_sem=recv_sems.at[1],
+            device_id=(to_wa, to_af),
+            device_id_type=MESH,
+        ).start()
+
+    each_partner(send_fourier)
+    four_recv[my_block] = four_send[my_wa]
+
     longitudes = first_lon + iota((1, lon_count), 1)
     in_row = (longitudes < points_int).astype(jnp.float32)
     usable = in_row * land_ref[...].astype(jnp.float32)
     soil_kinds = params_ref.shape[1]
-    plant_kinds = roots_ref.shape[0]
+    plant_kinds = roots_ref.shape[1]
     soil_hot = (iota((soil_kinds, lon_count), 0) == soil_ref[...]).astype(jnp.float32)
     plant_hot = (iota((plant_kinds, lon_count), 0) == plant_ref[...]).astype(jnp.float32)
     soil = dot(params_ref[...], soil_hot, 1, 0, HIGHEST)
     wilting = 0.04 + 0.1 * soil[0:1]
     capacity = 0.3 + 0.15 * soil[1:2]
     roots = roots_ref[...]
-    fractions = roots / jnp.sum(roots, axis=1, keepdims=True)
-    root_share = dot(fractions, plant_hot, 0, 0, HIGHEST)
+    fractions = roots / jnp.sum(roots, axis=0, keepdims=True)
+    root_share = dot(fractions, plant_hot, 1, 0, HIGHEST)
     moisture = water_ref[0]
     excess = moisture - wilting
     factor = jnp.clip(excess / (capacity - wilting), 0.0, 1.0)
@@ -292,8 +310,7 @@
     else:
         lax.fori_loop(0, chunks, analyse, 0)
 
-    def send_coeffs(step, carry):
-        to_wa, to_af = partner(step)
+    def send_coeffs(to_wa, to_af):
         pltpu.make_async_remote_copy(
             src_ref=coef_send.at[to_wa],
             dst_ref=coef_recv.at[my_block],
@@ -302,9 +319,8 @@
             device_id=(to_wa, to_af),
             device_id_type=MESH,
         ).start()
-        return carry
-
-    lax.fori_loop(1, devices, send_coeffs, 0)
+
+    each_partner(send_coeffs)
     coef_recv[my_block] = coef_send[my_wa]
     unfixed = demand * share_factor
     pltpu.make_async_copy(leg_bytes, leg_bytes, send_sems.at[0]).wait()
@@ -327,7 +343,7 @@
     offset = iota((rows8, n_local), 1) + my_af * n_local
     for s in range(slots):
         weighted = turned[s * rows8 : (s + 1) * rows8].astype(jnp.bfloat16)
-        result = dot(weighted, legendre_ref[s], 1, 1)
+        result = dot(weighted, legendre_ref[s], 1, 0)
         kept = offset < waves_total - wave_smem[my_wa * slots + s]
         spectral_ref[s] = jnp.where(kept, result, 0.0)
 
@@ -371,7 +387,7 @@
         out_specs=(vmem, vmem, vmem),
         scratch_shapes=[
             pltpu.VMEM((af_count, slots * lat_count, offsets), jnp.bfloat16),
-            pltpu.VMEM((slots, offsets, LANES), jnp.bfloat16),
+            pltpu.VMEM((slots, LANES, offsets), jnp.bfloat16),
             pltpu.VMEM((lat_count * SLOT_PAD, LANES), jnp.float32),
             pltpu.VMEM((lat_count, SLOT_PAD, LANES), jnp.bfloat16),
             pltpu.VMEM((devices, SLOT_PAD, LANES), jnp.bfloat16),
@@ -387,8 +403,8 @@
             vmem_limit_bytes=(48 if chunks > 1 else 16) * 1024 * 1024,
         ),
     )(
-        spectra,
-        legendre,
+        spectra.transpose(0, 2, 1),
+        legendre.transpose(0, 2, 1),
         wave_of_slot,
         wave_of_slot.reshape(1, waves_total),
         row_points,
@@ -398,7 +414,7 @@
         soil_type,
         plant_type,
         soil_params,
-        root_profile,
+        root_profile.T,
     )
 
 

time: 28.3 us -> 31 us (1.095)
  local copies, waits for them, and re-layouts: 4.25 us -> 6.92 us
    unnamed x20 -> x21, local copies, waits for them, and re-layouts: 4.25 us -> 6.92 us
where the time goes in v2:
time: 31 us; the launch traced here: 30.6 us
  Pallas kernels  21.6 us (70%)
  local copies, waits for them, and re-layouts  6.92 us (22%)
  between operations  2.01 us (6%)
    pallas_call x1, Pallas kernels, per_device(): pl.pallas_call(functools.partial(kernel, wa_count, af_count), out_shape=(...  21.6 us
    unnamed x21, local copies, waits for them, and re-layouts  6.92 us

profile of v2, /device:TPU:0, one launch (start us, length us, event | category | flops | bytes accessed | tf_op | source)
XLA Modules:
  0.0 30.6 jit_solution(16860353018158472168)
XLA Ops:
  0.6 0.0 copy-start.4
  1.3 0.0 copy-start.3
  2.0 0.0 copy-start.7
  2.0 0.0 copy-done.4
  2.0 0.0 copy-done.3
  2.0 0.6 %copy-done.7 = s32[80]{0:T(128)S(1)} copy-done((s32[80]{0:T(128)S(1)}, s32[80]{0:T(128)}, u32[]{:S(2)}) %copy-start.7) | copy-done | bytes 344
  2.6 0.0 copy-start
  2.6 0.9 %copy-done = bf16[10,80,32]{1,2,0:T(8,128)(2,1)S(1)} copy-done((bf16[10,80,32]{1,2,0:T(8,128)(2,1)S(1)}, bf16[10,80,32]{1,2,0:T(8,128)(2,1)}, u32[]{:S(2)}) %copy-start) | copy-done | bytes 51224
  3.5 0.0 copy-start.1
  3.5 0.7 %copy-done.1 = bf16[10,20,8]{1,2,0:T(8,128)(2,1)S(1)} copy-done((bf16[10,20,8]{1,2,0:T(8,128)(2,1)S(1)}, bf16[10,20,8]{1,2,0:T(8,128)(2,1)}, u32[]{:S(2)}) %copy-start.1) | copy-done | bytes 3224
  4.2 0.0 copy-start.2
  4.2 0.7 %copy-done.2 = f32[1,4,1280]{2,1,0:T(4,128)S(1)} copy-done((f32[1,4,1280]{2,1,0:T(4,128)S(1)}, f32[1,4,1280]{2,1,0:T(4,128)}, u32[]{:S(2)}) %copy-start.2) | copy-done | bytes 20504
  5.0 0.0 copy-start.5
  5.0 0.7 %copy-done.5 = s32[1,1280]{1,0:T(1,128)S(1)} copy-done((s32[1,1280]{1,0:T(1,128)S(1)}, s32[1,1280]{1,0:T(1,128)}, u32[]{:S(2)}) %copy-start.5) | copy-done | bytes 5144
  5.7 0.0 copy-start.6
  5.7 0.7 %copy-done.6 = f32[20,4]{0,1:T(4,128)S(1)} copy-done((f32[20,4]{0,1:T(4,128)S(1)}, f32[20,4]{0,1:T(4,128)}, u32[]{:S(2)}) %copy-start.6) | copy-done | bytes 344
  6.3 0.0 copy-start.8
  6.3 0.7 %copy-done.8 = f32[2,7]{1,0:T(2,128)S(1)} copy-done((f32[2,7]{1,0:T(2,128)S(1)}, f32[2,7]{1,0:T(2,128)}, u32[]{:S(2)}) %copy-start.8) | copy-done | bytes 80
  7.0 21.6 %shard_map.130 = (bf16[1,64,1280]{2,1,0:T(8,128)(2,1)S(1)}, f32[1,4,1280]{2,1,0:T(4,128)S(1)}, f32[10,8,20]{2,1,0:T(8,128)S(1)}) custom-call(bf16[10,32,80]{2,1,0:T(8,128)(2,1)S(1)} %bitcast.4, bf16[10,8,20]{2,1,0:T(8,128)(2,1)S(1)} %bitcast.5, s32[80]{0:T(128)S(1)} %copy-done.7, s32[1,80]{1,0:T(1,128)S(1)} %bitcast.7, s32[1]{0:T(128)S(6)} %copy.17.points_smem, ...), custom_call_target="tpu_custom_call" | custom-call | tf_op jit(solution)/shard_map/pallas_call | solution.py:379
  28.7 0.7 %copy.19 = bf16[1,64,1280]{2,1,0:T(8,128)(2,1)} copy(bf16[1,64,1280]{2,1,0:T(8,128)(2,1)S(1)} %get-tuple-element.6) | data formatting | bytes 327680
  29.3 0.6 %copy.20 = f32[1,4,1280]{2,1,0:T(4,128)} copy(f32[1,4,1280]{2,1,0:T(4,128)S(1)} %get-tuple-element.7) | data formatting | bytes 40960
  29.9 0.6 %copy.21 = f32[10,8,20]{2,1,0:T(8,128)} copy(f32[10,8,20]{2,1,0:T(8,128)S(1)} %get-tuple-element.8) | data formatting | bytes 12800
Async XLA Ops:
  0.6 1.3 %copy-start.4 = (s32[1,1280]{1,0:T(1,128)S(1)}, s32[1,1280]{1,0:T(1,128)}, u32[]{:S(2)}) copy-start(s32[1,1280]{1,0:T(1,128)} %soil_ref.1) | copy-start | bytes 15364
  1.3 0.7 %copy-start.3 = (s32[1,1280]{1,0:T(1,128)S(1)}, s32[1,1280]{1,0:T(1,128)}, u32[]{:S(2)}) copy-start(s32[1,1280]{1,0:T(1,128)} %land_ref.1) | copy-start | bytes 15364
  2.0 0.7 %copy-start.7 = (s32[80]{0:T(128)S(1)}, s32[80]{0:T(128)}, u32[]{:S(2)}) copy-start(s32[80]{0:T(128)} %wave_smem.1) | copy-start | bytes 964
  2.6 0.9 %copy-start = (bf16[10,80,32]{1,2,0:T(8,128)(2,1)S(1)}, bf16[10,80,32]{1,2,0:T(8,128)(2,1)}, u32[]{:S(2)}) copy-start(bf16[10,80,32]{1,2,0:T(8,128)(2,1)} %param.11) | copy-start | bytes 153604
  3.5 0.7 %copy-start.1 = (bf16[10,20,8]{1,2,0:T(8,128)(2,1)S(1)}, bf16[10,20,8]{1,2,0:T(8,128)(2,1)}, u32[]{:S(2)}) copy-start(bf16[10,20,8]{1,2,0:T(8,128)(2,1)} %param.12) | copy-start | bytes 9604
  4.2 0.7 %copy-start.2 = (f32[1,4,1280]{2,1,0:T(4,128)S(1)}, f32[1,4,1280]{2,1,0:T(4,128)}, u32[]{:S(2)}) copy-start(f32[1,4,1280]{2,1,0:T(4,128)} %water_ref.1) | copy-start | bytes 61444
  5.0 0.7 %copy-start.5 = (s32[1,1280]{1,0:T(1,128)S(1)}, s32[1,1280]{1,0:T(1,128)}, u32[]{:S(2)}) copy-start(s32[1,1280]{1,0:T(1,128)} %plant_ref.1) | copy-start | bytes 15364
  5.7 0.7 %copy-start.6 = (f32[20,4]{0,1:T(4,128)S(1)}, f32[20,4]{0,1:T(4,128)}, u32[]{:S(2)}) copy-start(f32[20,4]{0,1:T(4,128)} %param.21) | copy-start | bytes 964
  6.3 0.7 %copy-start.8 = (f32[2,7]{1,0:T(2,128)S(1)}, f32[2,7]{1,0:T(2,128)}, u32[]{:S(2)}) copy-start(f32[2,7]{1,0:T(2,128)} %params_ref.1) | copy-start | bytes 172

commit v3 on v2

--- a/solution.py
+++ b/solution.py
@@ -20,6 +20,7 @@
 CHUNK_WA = 8
 CHUNK = SLOT_PAD * CHUNK_WA
 LANES = 128
+VMEM_LIMIT = 56 * 1024 * 1024
 
 
 def dot(lhs, rhs, lhs_dim, rhs_dim, precision=None):
@@ -61,19 +62,19 @@
 def kernel(
     wa_count,
     af_count,
-    spectra_ref,
-    legendre_ref,
     wave_smem,
-    wave_ref,
     points_smem,
     weight_smem,
-    water_ref,
-    land_ref,
-    soil_ref,
-    plant_ref,
-    params_ref,
-    roots_ref,
-    grid_ref,
+    legendre_hbm,
+    spectra_hbm,
+    wave_hbm,
+    water_hbm,
+    land_hbm,
+    soil_hbm,
+    plant_hbm,
+    params_hbm,
+    roots_hbm,
+    grid_hbm,
     uptake_ref,
     spectral_ref,
     leg_all,
@@ -84,8 +85,19 @@
     tables,
     coef_send,
     coef_recv,
+    legendre_ref,
+    spectra_ref,
+    wave_ref,
+    water_ref,
+    land_ref,
+    soil_ref,
+    plant_ref,
+    params_ref,
+    roots_ref,
+    grid_ref,
     send_sems,
     recv_sems,
+    load_sems,
 ):
     slots, cols, offsets = spectra_ref.shape
     lat_count = legendre_ref.shape[1]
@@ -120,7 +132,27 @@
     def greet(to_wa, to_af):
         pl.semaphore_signal(barrier, inc=1, device_id=(to_wa, to_af), device_id_type=MESH)
 
+    loads = [
+        pltpu.make_async_copy(source, target, load_sems.at[number])
+        for number, (source, target) in enumerate(
+            (
+                (legendre_hbm, legendre_ref),
+                (spectra_hbm, spectra_ref),
+                (wave_hbm, wave_ref),
+                (water_hbm, water_ref),
+                (land_hbm, land_ref),
+                (soil_hbm, soil_ref),
+                (plant_hbm, plant_ref),
+                (params_hbm, params_ref),
+                (roots_hbm, roots_ref),
+            )
+        )
+    ]
+    loads[0].start()
     each_partner(greet)
+    for load in loads[1:]:
+        load.start()
+    loads[0].wait()
 
     place = (
         iota((n_local, offsets), 1) == iota((n_local, offsets), 0) + my_af * n_local
@@ -146,6 +178,8 @@
         ).start()
 
     placed[...] = jnp.zeros_like(placed)
+    for load in loads[1:]:
+        load.wait()
     for s in range(slots):
         placed[s, pl.ds(pl.multiple_of(my_af * cols, cols), cols), :] = spectra_ref[s]
     four_rows[...] = jnp.zeros_like(four_rows)
@@ -259,6 +293,8 @@
         fields = lax.fori_loop(0, chunks, synthesize, fields)
     rounded = (fields * in_row * (1.0 / math.sqrt(waves_total))).astype(jnp.bfloat16)
     grid_ref[0] = rounded
+    grid_write = pltpu.make_async_copy(grid_ref, grid_hbm, load_sems.at[len(loads)])
+    grid_write.start()
     values = rounded.astype(jnp.float32)
 
     def lowest(field):
@@ -348,6 +384,7 @@
         spectral_ref[s] = jnp.where(kept, result, 0.0)
 
     pltpu.make_async_copy(coef_bytes, coef_bytes, send_sems.at[2]).wait()
+    grid_write.wait()
 
 
 def per_device(
@@ -376,15 +413,27 @@
     assert wa_count % CHUNK_WA == 0 and lon_count % LANES == 0
     vmem = pl.BlockSpec(memory_space=pltpu.VMEM)
     smem = pl.BlockSpec(memory_space=pltpu.SMEM)
-    return pl.pallas_call(
+    operands = (
+        legendre.transpose(0, 2, 1),
+        spectra.transpose(0, 2, 1),
+        wave_of_slot.reshape(1, waves_total),
+        soil_water,
+        land_mask,
+        soil_type,
+        plant_type,
+        soil_params,
+        root_profile.T,
+    )
+    hbm = pl.BlockSpec(memory_space=pltpu.HBM)
+    results = pl.pallas_call(
         functools.partial(kernel, wa_count, af_count),
         out_shape=(
             jax.ShapeDtypeStruct((1, cols // 2 * af_count, lon_count), jnp.bfloat16),
             jax.ShapeDtypeStruct((1, SOIL_LAYERS, lon_count), jnp.float32),
             jax.ShapeDtypeStruct((slots, 2 * FLUXES, n_local), jnp.float32),
         ),
-        in_specs=[vmem, vmem, smem, vmem, smem, smem] + [vmem] * 6,
-        out_specs=(vmem, vmem, vmem),
+        in_specs=[smem] * 3 + [hbm] * len(operands),
+        out_specs=(hbm, vmem, vmem),
         scratch_shapes=[
             pltpu.VMEM((af_count, slots * lat_count, offsets), jnp.bfloat16),
             pltpu.VMEM((slots, LANES, offsets), jnp.bfloat16),
@@ -394,28 +443,39 @@
             pltpu.VMEM((chunks, 2 * CHUNK, lon_count), jnp.bfloat16),
             pltpu.VMEM((wa_count, 1, LANES), jnp.float32),
             pltpu.VMEM((devices, 1, LANES), jnp.float32),
+            *[pltpu.VMEM(operand.shape, operand.dtype) for operand in operands],
+            pltpu.VMEM((1, cols // 2 * af_count, lon_count), jnp.bfloat16),
             pltpu.SemaphoreType.DMA((3,)),
             pltpu.SemaphoreType.DMA((3,)),
+            pltpu.SemaphoreType.DMA((len(operands) + 1,)),
         ],
         compiler_params=pltpu.CompilerParams(
             collective_id=0,
             has_side_effects=True,
-            vmem_limit_bytes=(48 if chunks > 1 else 16) * 1024 * 1024,
+            vmem_limit_bytes=VMEM_LIMIT,
         ),
-    )(
-        spectra.transpose(0, 2, 1),
-        legendre.transpose(0, 2, 1),
-        wave_of_slot,
-        wave_of_slot.reshape(1, waves_total),
-        row_points,
-        row_weight,
-        soil_water,
-        land_mask,
-        soil_type,
-        plant_type,
-        soil_params,
-        root_profile.T,
-    )
+    )(wave_of_slot, row_points, row_weight, *operands)
+    return pl.pallas_call(
+        write_out,
+        out_shape=tuple(jax.ShapeDtypeStruct(r.shape, r.dtype) for r in results),
+        in_specs=[pl.BlockSpec(memory_space=pl.ANY)] * len(results),
+        out_specs=(hbm,) * len(results),
+        scratch_shapes=[pltpu.SemaphoreType.DMA((len(results),))],
+        compiler_params=pltpu.CompilerParams(vmem_limit_bytes=VMEM_LIMIT),
+    )(*results)
+
+
+def write_out(grid_in, uptake_in, spectral_in, grid_out, uptake_out, spectral_out, sems):
+    copies = [
+        pltpu.make_async_copy(source, target, sems.at[number])
+        for number, (source, target) in enumerate(
+            ((grid_in, grid_out), (uptake_in, uptake_out), (spectral_in, spectral_out))
+        )
+    ]
+    for copy in copies:
+        copy.start()
+    for copy in copies:
+        copy.wait()
 
 
 def solution(mesh):

time: 31 us -> 32.6 us (1.052)
  Pallas kernels: 21.6 us -> 30.4 us
  local copies, waits for them, and re-layouts: 6.92 us -> 0 us
    pallas_call x0 -> x1, Pallas kernels: none -> 7.95 us  [per_device(): pl.pallas_call(write_out, out_shape=tuple((jax.ShapeDtypeStruct(r.shape,...]
    unnamed x21 -> x0, local copies, waits for them, and re-layouts: 6.92 us -> none
    pallas_call x1, Pallas kernels: 21.6 us -> 22.5 us  [per_device(): pl.pallas_call(functools.partial(kernel, wa_count, af_count), out_shape=(...]
where the time goes in v3:
time: 32.6 us; the launch traced here: 32.4 us
  Pallas kernels  30.4 us (93%)
  between operations  1.93 us (6%)
    pallas_call x1, Pallas kernels, per_device(): pl.pallas_call(functools.partial(kernel, wa_count, af_count), out_shape=(...  22.5 us
    pallas_call x1, Pallas kernels, per_device(): pl.pallas_call(write_out, out_shape=tuple((jax.ShapeDtypeStruct(r.shape,...  7.95 us

profile of v3, /device:TPU:0, one launch (start us, length us, event | category | flops | bytes accessed | tf_op | source)
XLA Modules:
  0.0 32.4 jit_solution(15922140695324032453)
XLA Ops:
  1.9 22.5 %shard_map.130 = (bf16[1,64,1280]{2,1,0:T(8,128)(2,1)}, f32[1,4,1280]{2,1,0:T(4,128)}, f32[10,8,20]{2,1,0:T(8,128)}) custom-call(s32[80]{0:T(128)} %wave_smem.1, s32[1]{0:T(128)S(6)} %copy.14.points_smem, f32[1]{0:T(128)S(6)} %copy.15.weight_smem, bf16[10,8,20]{2,1,0:T(8,128)(2,1)} %bitcast.5, bf16[10,32,80]{2,1,0:T(8,128)(2,1)} %bitcast.4, ...), custom_call_target="tpu_custom_call" | custom-call | tf_op jit(solution)/shard_map/pallas_call | solution.py:428
  24.4 8.0 %shard_map.131 = (bf16[1,64,1280]{2,1,0:T(8,128)(2,1)}, f32[1,4,1280]{2,1,0:T(4,128)}, f32[10,8,20]{2,1,0:T(8,128)}) custom-call(bf16[1,64,1280]{2,1,0:T(8,128)(2,1)} %get-tuple-element.6.grid_in, f32[1,4,1280]{2,1,0:T(4,128)} %get-tuple-element.7.uptake_in, f32[10,8,20]{2,1,0:T(8,128)} %get-tuple-element.8.spectral_in), custom_call_target="tpu_custom_call" | custom-call | tf_op jit(solution)/shard_map/pallas_call | solution.py:458

commit v4 on v3

--- a/solution.py
+++ b/solution.py
@@ -425,7 +425,7 @@
         root_profile.T,
     )
     hbm = pl.BlockSpec(memory_space=pltpu.HBM)
-    results = pl.pallas_call(
+    return pl.pallas_call(
         functools.partial(kernel, wa_count, af_count),
         out_shape=(
             jax.ShapeDtypeStruct((1, cols // 2 * af_count, lon_count), jnp.bfloat16),
@@ -455,28 +455,6 @@
             vmem_limit_bytes=VMEM_LIMIT,
         ),
     )(wave_of_slot, row_points, row_weight, *operands)
-    return pl.pallas_call(
-        write_out,
-        out_shape=tuple(jax.ShapeDtypeStruct(r.shape, r.dtype) for r in results),
-        in_specs=[pl.BlockSpec(memory_space=pl.ANY)] * len(results),
-        out_specs=(hbm,) * len(results),
-        scratch_shapes=[pltpu.SemaphoreType.DMA((len(results),))],
-        compiler_params=pltpu.CompilerParams(vmem_limit_bytes=VMEM_LIMIT),
-    )(*results)
-
-
-def write_out(grid_in, uptake_in, spectral_in, grid_out, uptake_out, spectral_out, sems):
-    copies = [
-        pltpu.make_async_copy(source, target, sems.at[number])
-        for number, (source, target) in enumerate(
-            ((grid_in, grid_out), (uptake_in, uptake_out), (spectral_in, spectral_out))
-        )
-    ]
-    for copy in copies:
-        copy.start()
-    for copy in copies:
-        copy.wait()
-
 
 def solution(mesh):
     in_specs = (

time: 32.6 us -> 27.7 us (0.85)
  Pallas kernels: 30.4 us -> 22.5 us
  local copies, waits for them, and re-layouts: 0 us -> 3.01 us
    pallas_call x1 -> x0, Pallas kernels: 7.95 us -> none  [per_device(): pl.pallas_call(write_out, out_shape=tuple((jax.ShapeDtypeStruct(r.shape,...]
    unnamed x0 -> x7, local copies, waits for them, and re-layouts: none -> 3.01 us
where the time goes in v4:
time: 27.7 us; the launch traced here: 27.4 us
  Pallas kernels  22.5 us (81%)
  local copies, waits for them, and re-layouts  3.01 us (11%)
  between operations  1.94 us (7%)
    pallas_call x1, Pallas kernels, per_device(): pl.pallas_call(functools.partial(kernel, wa_count, af_count), out_shape=(...  22.5 us
    unnamed x7, local copies, waits for them, and re-layouts  3.01 us

profile of v4, /device:TPU:0, one launch (start us, length us, event | category | flops | bytes accessed | tf_op | source)
XLA Modules:
  0.0 27.4 jit_solution(13400442248606575508)
XLA Ops:
  1.9 22.5 %shard_map.130 = (bf16[1,64,1280]{2,1,0:T(8,128)(2,1)}, f32[1,4,1280]{2,1,0:T(4,128)}, f32[10,8,20]{2,1,0:T(8,128)}) custom-call(s32[80]{0:T(128)} %wave_smem.1, s32[1]{0:T(128)S(6)} %copy.17.points_smem, f32[1]{0:T(128)S(6)} %copy.18.weight_smem, bf16[10,8,20]{2,1,0:T(8,128)(2,1)} %bitcast.5, bf16[10,32,80]{2,1,0:T(8,128)(2,1)} %bitcast.4, ...), custom_call_target="tpu_custom_call" | custom-call | tf_op jit(solution)/shard_map/pallas_call | solution.py:428
  24.4 0.0 copy-start.1
  24.4 1.6 %copy.19 = bf16[1,64,1280]{2,1,0:T(8,128)(2,1)} copy(bf16[1,64,1280]{2,1,0:T(8,128)(2,1)} %get-tuple-element.6) | data formatting | bytes 327680
  26.0 0.0 copy-done.1
  26.0 0.0 copy-start
  26.0 0.6 %copy.20 = f32[1,4,1280]{2,1,0:T(4,128)} copy(f32[1,4,1280]{2,1,0:T(4,128)S(1)} %copy-done.1) | data formatting | bytes 40960
  26.6 0.2 copy-done
  26.8 0.6 %copy.21 = f32[10,8,20]{2,1,0:T(8,128)} copy(f32[10,8,20]{2,1,0:T(8,128)S(1)} %copy-done) | data formatting | bytes 12800
Async XLA Ops:
  24.4 1.6 %copy-start.1 = (f32[1,4,1280]{2,1,0:T(4,128)S(1)}, f32[1,4,1280]{2,1,0:T(4,128)}, u32[]{:S(2)}) copy-start(f32[1,4,1280]{2,1,0:T(4,128)} %get-tuple-element.7) | copy-start | bytes 61444
  26.0 0.8 %copy-start = (f32[10,8,20]{2,1,0:T(8,128)S(1)}, f32[10,8,20]{2,1,0:T(8,128)}, u32[]{:S(2)}) copy-start(f32[10,8,20]{2,1,0:T(8,128)} %get-tuple-element.8) | copy-start | bytes 19204
